TPU v7x, 32 devices: a whole 2x2x4 slice. The times are simulated.
32 devices in a mesh: band: 8 (over z, x), slab: 4 (over y, core).
Axes of the slice: x: 2, y: 2, z: 4, core: 2. Of those that a mesh axis runs over, the one named last changes fastest.
Arguments:
- orbitals: float32 [32, 128, 128, 128], P('band', 'slab'), may hold values from -6 to 6
- owner_band: int32 [4], replicated, may hold values from 0 to 7
- owner_slot: int32 [4], replicated, may hold values from 0 to 3
- g_mask: int32 [128, 128, 128], P(None, 'slab'), may hold values from 0 to 1, as said below
Outputs:
- exchange_action: float32 [32, 128, 128, 128], P('band', 'slab')
Inputs may be any that keep to these rules, and one draw needn't show every extreme that they name: `owner_band`: the band index of the device that holds source orbital j. `owner_slot`: the position of source orbital j among its owner's 4 orbitals. 1 where the kernel is kept and 0 where it is cut; the point of zero wave vector, g_mask[0, 0, 0], is always cut.
All inputs are finite; a program needn't handle non-finite values.
Results may differ from a plain program's by a relative error of at most 0.0003.
Values sent between devices are 32-bit elements; how exact they have to be, the bound alone decides.
A program may use at most 192 MiB of HBM per device.

v0:
```python
import math
import jax
import jax.numpy as jnp
from jax import lax
from jax.sharding import PartitionSpec as P

GRID = 128
coulomb_gain = 128.0 * math.pi


def broadcast(value, axis, source):
    kept = jnp.where(lax.axis_index(axis) == source, value, 0).astype(value.dtype)
    return lax.psum(kept, axis)


def cas_matrix(count):
    wave_index = jnp.arange(count, dtype=jnp.int32)
    products = wave_index[:, None] * wave_index[None, :] % count
    angles = 2.0 * math.pi / count * products.astype(jnp.float32)
    return jnp.cos(angles) + jnp.sin(angles)


def fold_index(wave_index):
    return jnp.where(wave_index < GRID // 2, wave_index, wave_index - GRID).astype(jnp.float32)


def transform_planes(field, cas_rows):
    highest = lax.Precision.HIGHEST
    field = jnp.einsum("oxyz,kz->oxyk", field, cas_rows, precision=highest)
    return jnp.einsum("oxyz,ky->oxkz", field, cas_rows, precision=highest)


def transform_first(field, cas_rows):
    return jnp.einsum("oxyz,kx->okyz", field, cas_rows, precision=lax.Precision.HIGHEST)


def fetch_source(orbitals, owner_band, owner_slot, which):
    local_copy = lax.dynamic_index_in_dim(orbitals, owner_slot[which], 0, keepdims=False)
    return broadcast(local_copy, "band", owner_band[which])


def per_device(orbitals, owner_band, owner_slot, g_mask):
    cas_rows = cas_matrix(GRID)
    columns_dev = g_mask.shape[1]
    full_index = jnp.arange(GRID, dtype=jnp.int32)
    column_index = lax.axis_index("slab") * columns_dev + jnp.arange(columns_dev, dtype=jnp.int32)
    first_sq = fold_index(full_index) ** 2
    second_sq = fold_index(column_index) ** 2
    squares = first_sq[:, None, None] + second_sq[None, :, None] + first_sq[None, None, :]
    coulomb = g_mask.astype(jnp.float32) * coulomb_gain / (squares + 1.0)
    inverse = 1.0 / (GRID * GRID * GRID)
    source_count = owner_band.shape[0]
    sources = jnp.stack(
        [fetch_source(orbitals, owner_band, owner_slot, which) for which in range(source_count)]
    )
    accumulated = jnp.zeros(orbitals.shape, jnp.float32)
    for which in range(source_count):
        source_field = sources[which]
        density = orbitals * source_field[None]
        spectrum = transform_planes(density, cas_rows)
        items = lax.all_to_all(spectrum, "slab", split_axis=2, concat_axis=1, tiled=True)
        weigh_spectrum = transform_first(items, cas_rows) * coulomb[None]
        potential = transform_first(weigh_spectrum, cas_rows)
        potential = lax.all_to_all(potential, "slab", split_axis=1, concat_axis=2, tiled=True)
        potential = transform_planes(potential, cas_rows) * inverse
        accumulated = accumulated - potential * source_field[None]
    return accumulated


def solution(mesh):
    return jax.shard_map(
        per_device,
        mesh=mesh,
        in_specs=(P("band", "slab", None, None), P(), P(), P(None, "slab", None)),
        out_specs=P("band", "slab", None, None),
        check_vma=False,
    )
```

profile of v0, /device:TPU:0, one launch (start us, length us, event | category | flops | bytes accessed | tf_op | source)
XLA Modules:
  0.0 1164.9 jit_solution(12261178417186420591)
XLA Ops:
  27.2 275.4 %all-reduce.3.cloned.1.call-done = (f32[32,128,128]{2,1,0:T(8,128)}, f32[32,128,128]{2,1,0:T(8,128)}, f32[32,128,128]{2,1,0:T(8,128)}, f32[32,128,128]{2,1,0:T(8,128)}) async-done(((f32[32,128,128]{2,1,0:T(8,128)}, f32[32,128,128]{2,1,0:T(8,128)}, f32[32,128,128]{2,1,0:T(8,128)}, f32[32,128,128]{2,1,0:T(8,128)}), (f32[32,128,128]{2,1,0:T(8,128)}, f32[32,128,128]{2,1,0:T(8,128)}, f32[32,128,128]{2,1,0:T(8,128)}, ...) | async-done | bytes 8388624 | tf_op jit(solution)/shard_map/psum | solution.py:13
  302.5 10.5 fusion.30
  336.4 10.0 fusion.27
  363.5 66.1 %all-to-all-done = f32[4,32,128,128]{3,1,0,2:T(8,128)} async-done(((f32[4,32,128,128]{3,1,0,2:T(8,128)}), f32[4,32,128,128]{3,1,0,2:T(8,128)}, u32[]{:S(2)}, u32[]{:S(2)}) %all-to-all-start) | async-done | bytes 8388640 | tf_op jit(solution)/shard_map/all_to_all | solution.py:61
  435.2 10.0 fusion.24
  462.7 65.7 %all-to-all-done.2 = f32[4,32,128,128]{3,1,0,2:T(8,128)} async-done(((f32[4,32,128,128]{3,1,0,2:T(8,128)}), f32[4,32,128,128]{3,1,0,2:T(8,128)}, u32[]{:S(2)}, u32[]{:S(2)}) %all-to-all-start.2) | async-done | bytes 8388640 | tf_op jit(solution)/shard_map/all_to_all | solution.py:61
  534.1 10.0 fusion.21
  561.2 66.1 %all-to-all-done.4 = f32[4,32,128,128]{3,1,0,2:T(8,128)} async-done(((f32[4,32,128,128]{3,1,0,2:T(8,128)}), f32[4,32,128,128]{3,1,0,2:T(8,128)}, u32[]{:S(2)}, u32[]{:S(2)}) %all-to-all-start.4) | async-done | bytes 8388640 | tf_op jit(solution)/shard_map/all_to_all | solution.py:61
  635.0 9.9 copy.30
  644.9 12.7 %fusion.18 = f32[128,4,32,128]{3,0,2,1:T(8,128)S(1)} fusion(f32[4,128,32,128]{3,2,1,0:T(8,128)S(1)} %bitcast.172), kind=kOutput, calls=%fused_computation.22 | convolution fusion | flops 3221471232 | bytes 16777216 | tf_op jit(solution)/shard_map/oxyz,kx->okyz/dot_general | solution.py:34
  657.5 9.4 fusion.40
  675.2 50.9 %all-to-all-done.6 = f32[4,32,128,128]{3,1,0,2:T(8,128)} async-done(((f32[4,32,128,128]{3,1,0,2:T(8,128)}), f32[4,32,128,128]{3,1,0,2:T(8,128)}, u32[]{:S(2)}, u32[]{:S(2)}) %all-to-all-start.6) | async-done | bytes 8388640 | tf_op jit(solution)/shard_map/all_to_all | solution.py:61
  731.9 9.9 copy.38
  741.8 12.6 %fusion.16 = f32[128,4,32,128]{3,0,2,1:T(8,128)S(1)} fusion(f32[4,128,32,128]{3,2,1,0:T(8,128)S(1)} %bitcast.173), kind=kOutput, calls=%fused_computation.20 | convolution fusion | flops 3221471232 | bytes 16777216 | tf_op jit(solution)/shard_map/oxyz,kx->okyz/dot_general | solution.py:34
  754.4 9.4 fusion.43
  771.9 53.0 %all-to-all-done.1 = f32[4,128,32,128]{3,2,0,1:T(8,128)} async-done(((f32[4,128,32,128]{3,2,0,1:T(8,128)}), f32[4,128,32,128]{3,2,0,1:T(8,128)}, u32[]{:S(2)}, u32[]{:S(2)}) %all-to-all-start.1) | async-done | bytes 8388640 | tf_op jit(solution)/shard_map/all_to_all | solution.py:64
  830.8 9.9 copy.45
  840.6 12.6 %fusion.14 = f32[128,4,32,128]{3,0,2,1:T(8,128)S(1)} fusion(f32[4,128,32,128]{3,2,1,0:T(8,128)S(1)} %bitcast.174), kind=kOutput, calls=%fused_computation.18 | convolution fusion | flops 3221471232 | bytes 16777216 | tf_op jit(solution)/shard_map/oxyz,kx->okyz/dot_general | solution.py:34
  853.3 9.4 fusion.46
  870.9 52.8 %all-to-all-done.3 = f32[4,128,32,128]{3,2,0,1:T(8,128)} async-done(((f32[4,128,32,128]{3,2,0,1:T(8,128)}), f32[4,128,32,128]{3,2,0,1:T(8,128)}, u32[]{:S(2)}, u32[]{:S(2)}) %all-to-all-start.3) | async-done | bytes 8388640 | tf_op jit(solution)/shard_map/all_to_all | solution.py:64
  929.5 9.9 copy.52
  939.4 12.7 %fusion.12 = f32[128,4,32,128]{3,0,2,1:T(8,128)S(1)} fusion(f32[4,128,32,128]{3,2,1,0:T(8,128)S(1)} %bitcast.175), kind=kOutput, calls=%fused_computation.16 | convolution fusion | flops 3221471232 | bytes 16777216 | tf_op jit(solution)/shard_map/oxyz,kx->okyz/dot_general | solution.py:34
  952.1 9.4 fusion.49
  969.6 53.0 %all-to-all-done.5 = f32[4,128,32,128]{3,2,0,1:T(8,128)} async-done(((f32[4,128,32,128]{3,2,0,1:T(8,128)}), f32[4,128,32,128]{3,2,0,1:T(8,128)}, u32[]{:S(2)}, u32[]{:S(2)}) %all-to-all-start.5) | async-done | bytes 8388640 | tf_op jit(solution)/shard_map/all_to_all | solution.py:64
  1051.8 10.2 fusion.80
  1062.0 10.0 fusion.78
  1072.0 8.8 fusion.72
  1080.9 10.1 fusion.70
  1099.6 10.3 fusion.62
  1109.9 11.6 all-to-all-done.7
  1125.9 9.4 fusion.56
  1135.3 22.2 %fusion = f32[4,32,128,128]{3,2,1,0:T(8,128)} fusion(f32[128,4,32,128]{3,0,2,1:T(8,128)} %fusion.62, f32[128,4,32,128]{3,0,2,1:T(8,128)} %fusion.70, f32[128,4,32,128]{3,0,2,1:T(8,128)} %fusion.78, f32[32,128,128]{2,1,0:T(8,128)S(1)} %copy-done.6, f32[32,128,128]{2,1,0:T(8,128)} %get-tuple-element.22, f32[32,128,128]{2,1,0:T(8,128)} %get-tuple-element.23, ...), kind=kOutput, calls=%fused_computation.1 | convolution fusion | flops 3238248448 | bytes 50331648 | tf_op jit(solution)/shard_map/oxyz,ky->oxkz/dot_general | solution.py:30
  (53 shorter events, 196.7 us)
Async XLA Ops:
  6.5 296.0 %all-reduce.3.cloned.1.call-start = ((), (), s32[]{:S(2)}) async-start(), calls=%async_computation.8 | async-start | bytes 16777216 | tf_op jit(solution)/shard_map/psum | solution.py:13
  330.6 5.8 copy-start
  330.6 99.0 %all-to-all-start = ((f32[4,32,128,128]{3,1,0,2:T(8,128)}), f32[4,32,128,128]{3,1,0,2:T(8,128)}, u32[]{:S(2)}, u32[]{:S(2)}) async-start(f32[4,32,128,128]{3,1,0,2:T(8,128)} %copy.28), calls=%async_computation | async-start | bytes 16777216 | tf_op jit(solution)/shard_map/all_to_all | solution.py:61
  363.5 71.7 %copy-start.3 = (f32[32,128,128]{2,1,0:T(8,128)S(1)}, f32[32,128,128]{2,1,0:T(8,128)}, u32[]{:S(2)}) copy-start(f32[32,128,128]{2,1,0:T(8,128)} %get-tuple-element.5) | copy-start | bytes 6291460
  429.5 98.9 %all-to-all-start.2 = ((f32[4,32,128,128]{3,1,0,2:T(8,128)}), f32[4,32,128,128]{3,1,0,2:T(8,128)}, u32[]{:S(2)}, u32[]{:S(2)}) async-start(f32[4,32,128,128]{3,1,0,2:T(8,128)} %copy.36), calls=%async_computation.2 | async-start | bytes 16777216 | tf_op jit(solution)/shard_map/all_to_all | solution.py:61
  462.7 71.4 %copy-start.5 = (f32[32,128,128]{2,1,0:T(8,128)S(1)}, f32[32,128,128]{2,1,0:T(8,128)}, u32[]{:S(2)}) copy-start(f32[32,128,128]{2,1,0:T(8,128)} %get-tuple-element.8) | copy-start | bytes 6291460
  528.4 98.9 %all-to-all-start.4 = ((f32[4,32,128,128]{3,1,0,2:T(8,128)}), f32[4,32,128,128]{3,1,0,2:T(8,128)}, u32[]{:S(2)}, u32[]{:S(2)}) async-start(f32[4,32,128,128]{3,1,0,2:T(8,128)} %copy.43), calls=%async_computation.4 | async-start | bytes 16777216 | tf_op jit(solution)/shard_map/all_to_all | solution.py:61
  561.2 71.9 %copy-start.7 = (s32[128,32,128]{2,1,0:T(8,128)S(1)}, s32[128,32,128]{2,1,0:T(8,128)}, u32[]{:S(2)}) copy-start(s32[128,32,128]{2,1,0:T(8,128)} %param.7) | copy-start | bytes 6291460
  627.3 98.8 %all-to-all-start.6 = ((f32[4,32,128,128]{3,1,0,2:T(8,128)}), f32[4,32,128,128]{3,1,0,2:T(8,128)}, u32[]{:S(2)}, u32[]{:S(2)}) async-start(f32[4,32,128,128]{3,1,0,2:T(8,128)} %copy.50), calls=%async_computation.6 | async-start | bytes 16777216 | tf_op jit(solution)/shard_map/all_to_all | solution.py:61
  726.1 98.8 %all-to-all-start.1 = ((f32[4,128,32,128]{3,2,0,1:T(8,128)}), f32[4,128,32,128]{3,2,0,1:T(8,128)}, u32[]{:S(2)}, u32[]{:S(2)}) async-start(f32[4,128,32,128]{3,2,0,1:T(8,128)} %copy.33), calls=%async_computation.1 | async-start | bytes 16777216 | tf_op jit(solution)/shard_map/all_to_all | solution.py:64
  824.9 98.9 %all-to-all-start.3 = ((f32[4,128,32,128]{3,2,0,1:T(8,128)}), f32[4,128,32,128]{3,2,0,1:T(8,128)}, u32[]{:S(2)}, u32[]{:S(2)}) async-start(f32[4,128,32,128]{3,2,0,1:T(8,128)} %copy.40), calls=%async_computation.3 | async-start | bytes 16777216 | tf_op jit(solution)/shard_map/all_to_all | solution.py:64
  923.8 98.8 %all-to-all-start.5 = ((f32[4,128,32,128]{3,2,0,1:T(8,128)}), f32[4,128,32,128]{3,2,0,1:T(8,128)}, u32[]{:S(2)}, u32[]{:S(2)}) async-start(f32[4,128,32,128]{3,2,0,1:T(8,128)} %copy.47), calls=%async_computation.5 | async-start | bytes 16777216 | tf_op jit(solution)/shard_map/all_to_all | solution.py:64
  969.6 58.8 %copy-start.4 = (f32[32,128,128]{2,1,0:T(8,128)S(1)}, f32[32,128,128]{2,1,0:T(8,128)}, u32[]{:S(2)}) copy-start(f32[32,128,128]{2,1,0:T(8,128)} %get-tuple-element.5) | copy-start | bytes 6291460
  1022.5 99.0 %all-to-all-start.7 = ((f32[4,128,32,128]{3,2,0,1:T(8,128)}), f32[4,128,32,128]{3,2,0,1:T(8,128)}, u32[]{:S(2)}, u32[]{:S(2)}) async-start(f32[4,128,32,128]{3,2,0,1:T(8,128)} %copy.54), calls=%async_computation.7 | async-start | bytes 16777216 | tf_op jit(solution)/shard_map/all_to_all | solution.py:64
  1028.4 4.1 copy-start.1
  1028.4 4.1 copy-start.2
  1125.9 9.4 copy-start.6
Sparse Core Ops, SparseCore 0:
  27.3 275.2 all-reduce.2
where the time goes:
time: 1170 us; the launch traced here: 1160 us
  waiting for transfers between devices  695 us (59%)
  matrix products  253 us (22%)
  local copies, waits for them, and re-layouts  132 us (11%)
  starting transfers between devices  46 us (4%)
  between operations  24.4 us (2%)
  other arithmetic  14.7 us (1%)
    psum x1, waiting for transfers between devices, broadcast(): return lax.psum(kept, axis)  275 us
    all_to_all x4, waiting for transfers between devices, per_device(): lax.all_to_all(spectrum, 'slab', split_axis=2, concat_axis=1, tiled=True)  249 us
    all_to_all x4, waiting for transfers between devices, per_device(): lax.all_to_all(potential, 'slab', split_axis=1, concat_axis=2, tiled=True)  170 us
    dot_general x8, matrix products, transform_first(): jnp.einsum('oxyz,kx->okyz', field, cas_rows, precision=lax.Precision.HIGH...  88.1 us
    dot_general x8, matrix products, transform_planes(): return jnp.einsum('oxyz,ky->oxkz', field, cas_rows, precision=highest)  87.7 us
    dot_general x8, matrix products, transform_planes(): field = jnp.einsum('oxyz,kz->oxyk', field, cas_rows, precision=highest)  77.6 us
    all_to_all x4, local copies, waits for them, and re-layouts, per_device(): lax.all_to_all(spectrum, 'slab', split_axis=2, concat_axis=1, tiled=True)  39.5 us
    transpose x4, local copies, waits for them, and re-layouts, transform_planes(): return jnp.einsum('oxyz,ky->oxkz', field, cas_rows, precision=highest)  34 us
  transfers between devices with their start and end apart: 9, of which 9 were waited for; matrix products, arithmetic and copies ran while one was open for 28% of the time, Pallas kernels for 0%

commit v1 on v0

--- a/solution.py
+++ b/solution.py
@@ -10,7 +10,8 @@
 
 def broadcast(value, axis, source):
     kept = jnp.where(lax.axis_index(axis) == source, value, 0).astype(value.dtype)
-    return lax.psum(kept, axis)
+    loads_enter = lambda array_in, dev_axis: lax.all_gather(array_in, dev_axis).sum(axis=0)
+    return loads_enter(kept, axis)
 
 
 def cas_matrix(count):

time: 1170 us -> 1530 us (1.31)
  waiting for transfers between devices: 695 us -> 1020 us
  other arithmetic: 14.7 us -> 49.8 us
    all_gather x0 -> x4, waiting for transfers between devices: none -> 786 us  [broadcast(): lax.all_gather(array_in, dev_axis).sum(axis=0)]
    psum x1 -> x0, waiting for transfers between devices: 275 us -> none  [broadcast(): return lax.psum(kept, axis)]
    all_to_all x4, waiting for transfers between devices: 249 us -> 49.1 us  [per_device(): lax.all_to_all(spectrum, 'slab', split_axis=2, concat_axis=1, tiled=True)]
    reduce_sum x0 -> x4, other arithmetic: none -> 32.4 us  [broadcast(): lax.all_gather(array_in, dev_axis).sum(axis=0)]
  transfers between devices with their start and end apart: 9 -> 12, of which waited for: 9 -> 9; matrix products, arithmetic and copies ran while one was open for 28% -> 25% of each run, Pallas kernels for 0% -> 0%
where the time goes in v1:
time: 1530 us; the launch traced here: 1520 us
  waiting for transfers between devices  1020 us (67%)
  matrix products  256 us (17%)
  local copies, waits for them, and re-layouts  132 us (9%)
  other arithmetic  49.8 us (3%)
  starting transfers between devices  46.9 us (3%)
  between operations  24 us (2%)
    all_gather x4, waiting for transfers between devices, broadcast(): lax.all_gather(array_in, dev_axis).sum(axis=0)  786 us
    all_to_all x4, waiting for transfers between devices, per_device(): lax.all_to_all(potential, 'slab', split_axis=1, concat_axis=2, tiled=True)  180 us
    dot_general x8, matrix products, transform_first(): jnp.einsum('oxyz,kx->okyz', field, cas_rows, precision=lax.Precision.HIGH...  87.8 us
    dot_general x8, matrix products, transform_planes(): return jnp.einsum('oxyz,ky->oxkz', field, cas_rows, precision=highest)  87.7 us
    dot_general x8, matrix products, transform_planes(): field = jnp.einsum('oxyz,kz->oxyk', field, cas_rows, precision=highest)  80.1 us
    all_to_all x4, waiting for transfers between devices, per_device(): lax.all_to_all(spectrum, 'slab', split_axis=2, concat_axis=1, tiled=True)  49.1 us
    all_to_all x4, local copies, waits for them, and re-layouts, per_device(): lax.all_to_all(spectrum, 'slab', split_axis=2, concat_axis=1, tiled=True)  40.2 us
    transpose x4, local copies, waits for them, and re-layouts, transform_planes(): return jnp.einsum('oxyz,ky->oxkz', field, cas_rows, precision=highest)  33.7 us
  transfers between devices with their start and end apart: 12, of which 9 were waited for; matrix products, arithmetic and copies ran while one was open for 25% of the time, Pallas kernels for 0%

profile of v1, /device:TPU:0, one launch (start us, length us, event | category | flops | bytes accessed | tf_op | source)
XLA Modules:
  0.0 1525.0 jit_solution(644770169376743500)
XLA Ops:
  29.2 228.4 %all-gather.11.cloned.1.call-done = f32[8,32,128,128]{3,2,1,0:T(8,128)} async-done(((f32[1,32,128,128]{3,2,1,0:T(8,128)}), f32[8,32,128,128]{3,2,1,0:T(8,128)}) %all-gather.11.cloned.1.call-update) | async-done | bytes 16777232 | tf_op jit(solution)/shard_map/all_gather | solution.py:13
  265.3 11.5 fusion.21
  299.6 185.9 %all-gather.9.cloned.1.call-done = f32[8,32,128,128]{3,2,1,0:T(8,128)} async-done(((f32[1,32,128,128]{3,2,1,0:T(8,128)}), f32[8,32,128,128]{3,2,1,0:T(8,128)}) %all-gather.9.cloned.1.call-update) | async-done | bytes 16777232 | tf_op jit(solution)/shard_map/all_gather | solution.py:13
  493.3 11.8 fusion.24
  527.9 185.6 %all-gather.7.cloned.1.call-done = f32[8,32,128,128]{3,2,1,0:T(8,128)} async-done(((f32[1,32,128,128]{3,2,1,0:T(8,128)}), f32[8,32,128,128]{3,2,1,0:T(8,128)}) %all-gather.7.cloned.1.call-update) | async-done | bytes 16777232 | tf_op jit(solution)/shard_map/all_gather | solution.py:13
  721.2 11.2 fusion.27
  755.2 186.1 %all-gather.5.cloned.1.call-done = f32[8,32,128,128]{3,2,1,0:T(8,128)} async-done(((f32[1,32,128,128]{3,2,1,0:T(8,128)}), f32[8,32,128,128]{3,2,1,0:T(8,128)}) %all-gather.5.cloned.1.call-update) | async-done | bytes 16777232 | tf_op jit(solution)/shard_map/all_gather | solution.py:13
  941.3 9.1 reduce_sum.36
  950.4 10.3 fusion.30
  987.2 10.6 copy.52
  997.8 12.8 fusion.12
  1010.6 9.2 fusion.49
  1027.9 49.1 %all-to-all-done = f32[4,32,128,128]{3,1,0,2:T(8,128)} async-done(((f32[4,32,128,128]{3,1,0,2:T(8,128)}), f32[4,32,128,128]{3,1,0,2:T(8,128)}, u32[]{:S(2)}, u32[]{:S(2)}) %all-to-all-start) | async-done | bytes 8388640 | tf_op jit(solution)/shard_map/all_to_all | solution.py:62
  1083.1 9.9 copy.45
  1092.9 12.8 fusion.14
  1105.7 9.3 fusion.46
  1123.3 52.5 %all-to-all-done.7 = f32[4,128,32,128]{3,2,0,1:T(8,128)} async-done(((f32[4,128,32,128]{3,2,0,1:T(8,128)}), f32[4,128,32,128]{3,2,0,1:T(8,128)}, u32[]{:S(2)}, u32[]{:S(2)}) %all-to-all-start.7) | async-done | bytes 8388640 | tf_op jit(solution)/shard_map/all_to_all | solution.py:65
  1181.9 9.9 copy.38
  1191.8 12.8 fusion.16
  1204.6 9.3 fusion.43
  1222.0 52.6 %all-to-all-done.5 = f32[4,128,32,128]{3,2,0,1:T(8,128)} async-done(((f32[4,128,32,128]{3,2,0,1:T(8,128)}), f32[4,128,32,128]{3,2,0,1:T(8,128)}, u32[]{:S(2)}, u32[]{:S(2)}) %all-to-all-start.5) | async-done | bytes 8388640 | tf_op jit(solution)/shard_map/all_to_all | solution.py:65
  1280.7 9.9 copy.30
  1290.6 12.6 fusion.18
  1303.2 9.0 fusion.40
  1320.4 53.1 %all-to-all-done.3 = f32[4,128,32,128]{3,2,0,1:T(8,128)} async-done(((f32[4,128,32,128]{3,2,0,1:T(8,128)}), f32[4,128,32,128]{3,2,0,1:T(8,128)}, u32[]{:S(2)}, u32[]{:S(2)}) %all-to-all-start.3) | async-done | bytes 8388640 | tf_op jit(solution)/shard_map/all_to_all | solution.py:65
  1404.4 9.3 fusion.56
  1422.3 10.3 fusion.62
  1441.2 10.1 fusion.70
  1451.3 21.3 %all-to-all-done.1 = f32[4,128,32,128]{3,2,0,1:T(8,128)} async-done(((f32[4,128,32,128]{3,2,0,1:T(8,128)}), f32[4,128,32,128]{3,2,0,1:T(8,128)}, u32[]{:S(2)}, u32[]{:S(2)}) %all-to-all-start.1) | async-done | bytes 8388640 | tf_op jit(solution)/shard_map/all_to_all | solution.py:65
  1477.1 8.8 fusion.80
  1485.9 10.1 fusion.78
  1496.0 22.2 %fusion = f32[4,32,128,128]{3,2,1,0:T(8,128)} fusion(f32[128,4,32,128]{3,0,2,1:T(8,128)} %fusion.62, f32[128,4,32,128]{3,0,2,1:T(8,128)} %fusion.70, f32[128,4,32,128]{3,0,2,1:T(8,128)} %fusion.78, f32[32,128,128]{2,1,0:T(8,128)} %broadcast_multiply_fusion, f32[32,128,128]{2,1,0:T(8,128)} %broadcast_multiply_fusion.1, ...), kind=kOutput, calls=%fused_computation.1 | convolution fusion | flops 3238248448 | bytes 50331648 | tf_op jit(solution)/shard_map/oxyz,ky->oxkz/dot_general | solution.py:31
  (72 shorter events, 233.5 us)
Async XLA Ops:
  6.5 251.0 %all-gather.11.cloned.1.call-start = ((), (), s32[]{:S(2)}) async-start(), calls=%async_computation.11 | async-start | bytes 18874368 | tf_op jit(solution)/shard_map/all_gather | solution.py:13
  27.1 458.4 %all-gather.9.cloned.1.call-start = ((), (), s32[]{:S(2)}) async-start(), calls=%async_computation.10 | async-start | bytes 18874368 | tf_op jit(solution)/shard_map/all_gather | solution.py:13
  27.9 685.6 %all-gather.7.cloned.1.call-start = ((), (), s32[]{:S(2)}) async-start(), calls=%async_computation.9 | async-start | bytes 18874368 | tf_op jit(solution)/shard_map/all_gather | solution.py:13
  28.6 912.7 %all-gather.5.cloned.1.call-start = ((), (), s32[]{:S(2)}) async-start(), calls=%async_computation.8 | async-start | bytes 18874368 | tf_op jit(solution)/shard_map/all_gather | solution.py:13
  265.3 11.6 copy-start
  293.9 228.3 %all-to-all-start.6 = ((f32[4,32,128,128]{3,1,0,2:T(8,128)}), f32[4,32,128,128]{3,1,0,2:T(8,128)}, u32[]{:S(2)}, u32[]{:S(2)}) async-start(f32[4,32,128,128]{3,1,0,2:T(8,128)} %copy.50), calls=%async_computation.6 | async-start | bytes 16777216 | tf_op jit(solution)/shard_map/all_to_all | solution.py:62
  493.3 11.8 copy-start.2
  522.3 227.2 %all-to-all-start.4 = ((f32[4,32,128,128]{3,1,0,2:T(8,128)}), f32[4,32,128,128]{3,1,0,2:T(8,128)}, u32[]{:S(2)}, u32[]{:S(2)}) async-start(f32[4,32,128,128]{3,1,0,2:T(8,128)} %copy.43), calls=%async_computation.4 | async-start | bytes 16777216 | tf_op jit(solution)/shard_map/all_to_all | solution.py:62
  749.5 228.7 %all-to-all-start.2 = ((f32[4,32,128,128]{3,1,0,2:T(8,128)}), f32[4,32,128,128]{3,1,0,2:T(8,128)}, u32[]{:S(2)}, u32[]{:S(2)}) async-start(f32[4,32,128,128]{3,1,0,2:T(8,128)} %copy.36), calls=%async_computation.2 | async-start | bytes 16777216 | tf_op jit(solution)/shard_map/all_to_all | solution.py:62
  978.1 98.9 %all-to-all-start = ((f32[4,32,128,128]{3,1,0,2:T(8,128)}), f32[4,32,128,128]{3,1,0,2:T(8,128)}, u32[]{:S(2)}, u32[]{:S(2)}) async-start(f32[4,32,128,128]{3,1,0,2:T(8,128)} %copy.28), calls=%async_computation | async-start | bytes 16777216 | tf_op jit(solution)/shard_map/all_to_all | solution.py:62
  987.1 23.4 %copy-start.4 = (f32[128,32,128]{2,0,1:T(8,128)}, f32[128,32,128]{2,0,1:T(8,128)S(1)}, u32[]{:S(2)}) copy-start(f32[128,32,128]{2,0,1:T(8,128)S(1)} %copy.32) | copy-start | bytes 6291460
  1077.0 98.8 %all-to-all-start.7 = ((f32[4,128,32,128]{3,2,0,1:T(8,128)}), f32[4,128,32,128]{3,2,0,1:T(8,128)}, u32[]{:S(2)}, u32[]{:S(2)}) async-start(f32[4,128,32,128]{3,2,0,1:T(8,128)} %copy.54), calls=%async_computation.7 | async-start | bytes 16777216 | tf_op jit(solution)/shard_map/all_to_all | solution.py:65
  1092.9 12.8 copy-start.5
  1175.8 98.9 %all-to-all-start.5 = ((f32[4,128,32,128]{3,2,0,1:T(8,128)}), f32[4,128,32,128]{3,2,0,1:T(8,128)}, u32[]{:S(2)}, u32[]{:S(2)}) async-start(f32[4,128,32,128]{3,2,0,1:T(8,128)} %copy.47), calls=%async_computation.5 | async-start | bytes 16777216 | tf_op jit(solution)/shard_map/all_to_all | solution.py:65
  1191.8 12.8 copy-start.6
  1274.7 98.8 %all-to-all-start.3 = ((f32[4,128,32,128]{3,2,0,1:T(8,128)}), f32[4,128,32,128]{3,2,0,1:T(8,128)}, u32[]{:S(2)}, u32[]{:S(2)}) async-start(f32[4,128,32,128]{3,2,0,1:T(8,128)} %copy.40), calls=%async_computation.3 | async-start | bytes 16777216 | tf_op jit(solution)/shard_map/all_to_all | solution.py:65
  1290.6 12.6 copy-start.7
  1373.5 99.2 %all-to-all-start.1 = ((f32[4,128,32,128]{3,2,0,1:T(8,128)}), f32[4,128,32,128]{3,2,0,1:T(8,128)}, u32[]{:S(2)}, u32[]{:S(2)}) async-start(f32[4,128,32,128]{3,2,0,1:T(8,128)} %copy.33), calls=%async_computation.1 | async-start | bytes 16777216 | tf_op jit(solution)/shard_map/all_to_all | solution.py:65
  1379.5 4.8 copy-start.3
  1379.5 6.3 copy-start.1
  1404.4 9.3 copy-start.8
  1485.9 10.1 copy-start.9
Sparse Core Ops, SparseCore 0:
  27.2 230.2 all-gather.10
  259.7 225.7 all-gather.8
  487.6 225.7 all-gather.6
  715.4 225.7 all-gather.4
